TPU v7x, 1024 devices: a whole 8x8x8 slice. The times are simulated.
1024 devices in a mesh: blk: 32 (over y_lo, z), rep: 32 (over x, y_hi, core).
Axes of the slice: x: 8, y: 8 (y_hi: 2, y_lo: 4; y = y_hi * 4 + y_lo), z: 8, core: 2. Of those that a mesh axis runs over, the one named last changes fastest.
Arguments:
- features: bfloat16 [131072, 128], P(('blk', 'rep')), may hold values from -6 to 6
- weight: bfloat16 [128, 256], replicated, may hold values from -0.5 to 0.5
- cotangent: bfloat16 [131072, 256], P(('blk', 'rep')), may hold values from -6 to 6
- tile_vals: bfloat16 [32, 32, 32, 2, 128, 128], P('blk', 'rep'), may hold values from -0.09375 to 0.09375
- tile_row: int32 [32, 32, 32, 2], P('blk', 'rep'), may hold values from 0 to 31
- tile_count: int32 [32, 32, 32], P('blk', 'rep'), may hold values from 0 to 2, as said below
Outputs:
- activations: bfloat16 [131072, 256], P(('blk', 'rep'))
- feature_grad: bfloat16 [131072, 128], P(('blk', 'rep'))
- weight_grad: float32 [128, 256], replicated
Inputs may be any that keep to these rules, and one draw needn't show every extreme that they name: tile_count equals 2 wherever the column block j equals the row block b.
All inputs are finite; a program needn't handle non-finite values.
Results may differ from a plain program's by a relative error of at most 0.03.
Values may be sent and summed in bfloat16 or wider, within the bound.
No kernel may reach another device: no remote copies, remote signals or barrier semaphores. Data moves between devices by JAX's collectives and lax.ppermute only.
A program may use at most 32 MiB of HBM per device.

v0:
```python
import functools

import jax
import jax.numpy as jnp
from jax import lax
from jax.experimental import pallas as pl
from jax.experimental.pallas import tpu as pltpu
from jax.sharding import PartitionSpec as P

VMEM = pl.BlockSpec(memory_space=pltpu.VMEM)
SMEM = pl.BlockSpec(memory_space=pltpu.SMEM)
F32 = jnp.float32
BF16 = jnp.bfloat16


def block_of(near, far, blocks):
    y_near, z_near = divmod(near, 2)
    y_far, z_far = divmod(far, blocks // 8)
    return ((y_far * 2 + y_near) * (blocks // 8) + z_far) * 2 + z_near


def matmul(a, b):
    return jnp.dot(a, b, preferred_element_type=F32)


def spread(block_ref, copies_ref):
    for k in range(copies_ref.shape[0]):
        copies_ref[k] = block_ref[...]


def forward_tiles(rows_ref, counts_ref, features_ref, tiles_ref, kept_ref, sent_ref, total):
    rep = lax.axis_index("rep")
    blocks, slots, side, _ = tiles_ref.shape
    total[...] = jnp.zeros_like(total)
    for near in range(features_ref.shape[0]):
        for far in range(features_ref.shape[1]):
            j = block_of(near, far, blocks)
            product = matmul(tiles_ref[j].reshape(slots * side, side), features_ref[near, far])
            for slot in range(slots):
                row = rows_ref[slot, j]
                term = product[slot * side : (slot + 1) * side]
                total[lax.rem(row + rep, 2), row // 2] += jnp.where(slot < counts_ref[j], term, 0.0)
    kept_ref[...] = total[0]
    sent_ref[...] = total[1].astype(sent_ref.dtype)


def sum_parts(parts_ref, copies_ref):
    for place in range(2):
        total = parts_ref[place].astype(F32)
        for g in range(place + 2, parts_ref.shape[0], 2):
            total += parts_ref[g].astype(F32)
        copies_ref[place] = total.astype(BF16)
        copies_ref[place + 2] = total.astype(BF16)


def dense_layer(
    halves_ref, weight_ref, cotangent_ref, partner_ref, activations_ref, outgoing_ref
):
    side = cotangent_ref.shape[0]
    first = lax.rem(lax.axis_index("rep") // 2, 2) == 0
    aggregated = jnp.concatenate(
        [halves_ref[k].astype(F32) + halves_ref[k + 2].astype(F32) for k in range(2)], axis=0
    ).astype(BF16)
    cotangent, partner = cotangent_ref[...].astype(F32), partner_ref[...].astype(F32)
    cotangent = jnp.concatenate(
        [jnp.where(first, cotangent, partner), jnp.where(first, partner, cotangent)], axis=0
    )
    weight = weight_ref[...]
    pre = matmul(aggregated, weight)
    sigma = jax.nn.sigmoid(pre)
    activations = pre * sigma
    activations_ref[...] = jnp.where(first, activations[:side], activations[side:]).astype(BF16)
    grad_pre = (cotangent * sigma * (1.0 + pre * (1.0 - sigma))).astype(BF16)
    grad_agg = lax.dot_general(
        weight, grad_pre, (((1,), (1,)), ((), ())), preferred_element_type=F32
    ).astype(BF16)
    term = lax.dot_general(
        aggregated, grad_pre, (((0,), (0,)), ((), ())), preferred_element_type=F32
    )
    pieces = [
        term[top : top + 8, left : left + side]
        for top in range(0, term.shape[0], 8)
        for left in range(0, term.shape[1], side)
    ]
    count = len(pieces) // outgoing_ref.shape[0]
    for x in range(outgoing_ref.shape[0]):
        outgoing_ref[x, :side] = grad_agg[:, :side]
        outgoing_ref[x, side : 2 * side] = grad_agg[:, side:]
        lines = jnp.concatenate(pieces[x * count : (x + 1) * count], axis=0)
        outgoing_ref[x, 2 * side :] = lines.astype(BF16)


def backward_tiles(rows_ref, counts_ref, own_ref, other_ref, tiles_ref, outgoing_ref):
    rep = lax.axis_index("rep")
    blocks, slots, side, _ = tiles_ref.shape
    nears = outgoing_ref.shape[0]
    fars = blocks // nears
    grads = 2 * side
    own_sum, other_sum = own_ref[0, grads:].astype(F32), other_ref[0, grads:].astype(F32)
    for x in range(1, own_ref.shape[0]):
        own_sum += own_ref[x, grads:].astype(F32)
        other_sum += other_ref[x, grads:].astype(F32)
    carried = (own_sum + other_sum).astype(BF16)
    for near in range(nears):
        for far in range(fars):
            j = block_of(near, far, blocks)
            picked = []
            for slot in range(slots):
                row = rows_ref[slot, j]
                x = row // 4
                nodes = pl.ds(pl.multiple_of(lax.rem(row // 2, 2) * side, side), side)
                use_own = lax.rem(row + rep, 2) == 0
                block = jnp.where(use_own, own_ref[x, nodes], other_ref[x, nodes])
                picked.append(jnp.where(slot < counts_ref[j], block, jnp.zeros_like(block)))
            term = matmul(jnp.concatenate(picked, axis=1), tiles_ref[j].reshape(slots * side, side))
            outgoing_ref[near, far * side : (far + 1) * side] = term.astype(BF16)
        outgoing_ref[near, fars * side :] = carried


def relay_terms(arrived_ref, outgoing_ref):
    nears, _, side = arrived_ref.shape
    fars = outgoing_ref.shape[0]
    total = arrived_ref[0].astype(F32)
    for k in range(1, nears):
        total += arrived_ref[k].astype(F32)
    total = total.astype(BF16)
    for g in range(fars):
        outgoing_ref[g, :side] = total[g * side : (g + 1) * side]
        outgoing_ref[g, side:] = total[fars * side :]


def final_sums(parts_ref, feature_grad_ref, weight_ref):
    fars, _, side = parts_ref.shape
    total = parts_ref[0].astype(F32)
    for k in range(1, fars):
        total += parts_ref[k].astype(F32)
    feature_grad_ref[...] = total[:side].T.astype(BF16)
    for x in range(weight_ref.shape[0]):
        weight_ref[x] = total[side:]


def call(kernel, inputs, outputs, scratch=()):
    return pl.pallas_call(
        kernel,
        out_shape=outputs,
        in_specs=inputs,
        out_specs=[VMEM] * len(outputs),
        scratch_shapes=scratch,
        compiler_params=pltpu.CompilerParams(vmem_limit_bytes=32 * 2**20),
    )


def local(blocks, replicas, features, weight, cotangent, tile_vals, tile_row, tile_count):
    def shape(*dims, dtype=BF16):
        return jax.ShapeDtypeStruct(dims, dtype)

    side, width = features.shape
    hidden = weight.shape[1]
    nears, fars = 4, blocks // 4
    groups, x_size = replicas // 2, replicas // 4
    lines = weight.size // x_size // side
    tiles, rows, counts = tile_vals[0, 0], tile_row[0, 0].T, tile_count[0, 0]

    near_blocks = [[block_of(k, g, blocks) for k in range(nears)] for g in range(fars)]
    far_blocks = [[block_of(k, g, blocks) for g in range(fars)] for k in range(nears)]
    y_pairs = [[4 * x + c, 4 * x + 2 + c] for x in range(x_size) for c in range(2)]
    along_x = [[4 * x + k for x in range(x_size)] for k in range(4)]
    swap = [(r, r ^ 1) for r in range(replicas)]
    swap_y = [(r, r ^ 2) for r in range(replicas)]

    def exchange(block, axis, index_groups):
        return lax.all_to_all(block, axis, 0, 0, axis_index_groups=index_groups, tiled=True)

    with jax.named_scope("partner_cotangent"):
        partner = lax.ppermute(cotangent, "rep", swap_y)
    with jax.named_scope("gather_features"):
        (copies,) = call(spread, [VMEM], [shape(fars, side, width)])(features)
        band = exchange(copies, "blk", far_blocks)
        (copies,) = call(spread, [VMEM], [shape(nears, fars, side, width)])(band)
        gathered = exchange(copies, "blk", near_blocks)
    kept, sent = call(
        forward_tiles,
        [SMEM, SMEM, VMEM, VMEM],
        [shape(groups, side, width, dtype=F32), shape(groups, side, width)],
        [pltpu.VMEM((2, groups, side, width), F32)],
    )(rows, counts, gathered, tiles)
    with jax.named_scope("sum_partials"):
        pair = (kept + lax.ppermute(sent, "rep", swap).astype(F32)).astype(BF16)
        parts = exchange(pair, "rep", along_x)
        (copies,) = call(sum_parts, [VMEM], [shape(4, side, width)])(parts)
        halves = exchange(copies, "rep", y_pairs)
    activations, outgoing = call(
        dense_layer,
        [VMEM] * 4,
        [shape(side, hidden), shape(x_size, 2 * side + lines, width)],
    )(halves, weight, cotangent, partner)
    with jax.named_scope("gather_grads"):
        own = exchange(outgoing, "rep", along_x)
        other = lax.ppermute(own, "rep", swap)
    (terms,) = call(
        backward_tiles,
        [SMEM, SMEM, VMEM, VMEM, VMEM],
        [shape(nears, fars * side + lines, width)],
    )(rows, counts, own, other, tiles)
    with jax.named_scope("sum_terms"):
        arrived = exchange(terms, "blk", near_blocks)
        (terms,) = call(relay_terms, [VMEM], [shape(fars, side + lines, width)])(arrived)
        arrived = exchange(terms, "blk", far_blocks)
    feature_grad, piece = call(
        final_sums,
        [VMEM],
        [shape(side, width), shape(x_size, lines, width, dtype=F32)],
    )(arrived)
    with jax.named_scope("gather_weight_grad"):
        pieces = exchange(piece, "rep", along_x).reshape(-1, hidden // side, 8, side)
    weight_grad = pieces.transpose(0, 2, 1, 3).reshape(weight.shape)
    return activations, feature_grad, weight_grad


def solution(mesh):
    in_specs = (
        P(("blk", "rep"), None),
        P(),
        P(("blk", "rep"), None),
        P("blk", "rep", None, None, None, None),
        P("blk", "rep", None, None),
        P("blk", "rep", None),
    )
    out_specs = (P(("blk", "rep"), None), P(("blk", "rep"), None), P())
    step = functools.partial(local, mesh.shape["blk"], mesh.shape["rep"])
    return jax.shard_map(step, mesh=mesh, in_specs=in_specs, out_specs=out_specs, check_vma=False)
```

profile of v0, /device:TPU:2, one launch (start us, length us, event | category | flops | bytes accessed | tf_op | source)
XLA Modules:
  0.0 170.4 jit_solution(1678484494141667664)
XLA Ops:
  0.6 0.0 copy-start.3
  0.6 0.7 copy-done.3
  1.4 31.0 %all_to_all.40.block_ref = bf16[8,128,128]{2,1,0:T(8,128)(2,1)S(1)} all-to-all(bf16[8,128,128]{2,1,0:T(8,128)(2,1)S(1)} %gather_features.2), channel_id=1, replica_groups={{0,64,128,192,512,576,640,704},{32,96,160,224,544,608,672,736},{256,320..., dimensions={0} | all-to-all | bytes 524288 | tf_op jit(solution)/shard_map/gather_features/all_to_all | solution.py:172
  32.5 0.1 gather_features.3
  32.6 0.0 copy-start
  32.6 0.0 copy-start.4
  32.6 0.0 copy-start.5
  32.6 14.8 %all_to_all.41.features_ref = bf16[4,8,128,128]{3,2,1,0:T(8,128)(2,1)S(1)} all-to-all(bf16[4,8,128,128]{3,2,1,0:T(8,128)(2,1)S(1)} %gather_features.3), channel_id=1, replica_groups={{0,32,256,288},{64,96,320,352},{128,160,384,416},{192,224,448,480},{512..., dimensions={0} | all-to-all | bytes 2097152 | tf_op jit(solution)/shard_map/gather_features/all_to_all | solution.py:172
  47.5 0.0 copy-done.4
  47.5 1.6 shard_map.85
  49.1 1.9 %collective-permute-start = (bf16[16,128,128]{2,1,0:T(8,128)(2,1)S(1)}, bf16[16,128,128]{2,1,0:T(8,128)(2,1)S(1)}, u32[]{:S(2)}, u32[]{:S(2)}) collective-permute-start(bf16[16,128,128]{2,1,0:T(8,128)(2,1)S(1)} %get-tuple-element.10), channel_id=1, source_target_pairs={{0,1},{1,0},{2,3},{3,2},{4,5},{5,4},{6,7},{7,6},{8,9},{9,8},{10,11... | collective-permute-start | bytes 1572872 | tf_op jit(solution)/shard_map/sum_partials/ppermute | solution.py:188
  51.0 1.9 %collective-permute-done = bf16[16,128,128]{2,1,0:T(8,128)(2,1)S(1)} collective-permute-done((bf16[16,128,128]{2,1,0:T(8,128)(2,1)S(1)}, bf16[16,128,128]{2,1,0:T(8,128)(2,1)S(1)}, u32[]{:S(2)}, u32[]{:S(2)}) %collective-permute-start) | collective-permute-done | bytes 524320 | tf_op jit(solution)/shard_map/sum_partials/ppermute | solution.py:188
  52.9 0.1 add_convert_fusion
  53.0 0.0 copy-start.2
  53.0 0.0 copy-start.1
  53.1 23.6 %all_to_all.42.parts_ref = bf16[16,128,128]{2,1,0:T(8,128)(2,1)S(1)} all-to-all(bf16[16,128,128]{2,1,0:T(8,128)(2,1)S(1)} %add_convert_fusion), channel_id=1, replica_groups={{0,4,8,12,16,20,24,28},{1,5,9,13,17,21,25,29},{2,6,10,14,18,22,26,30},{..., dimensions={0} | all-to-all | bytes 1048576 | tf_op jit(solution)/shard_map/sum_partials/all_to_all | solution.py:172
  76.6 0.7 sum_partials.1
  77.3 7.6 %all-to-all-start.3 = ((bf16[4,128,128]{2,1,0:T(8,128)(2,1)}), bf16[4,128,128]{2,1,0:T(8,128)(2,1)S(1)}, u32[]{:S(2)}, u32[]{:S(2)}) async-start(bf16[4,128,128]{2,1,0:T(8,128)(2,1)} %sum_partials.1), calls=%async_computation.3 | async-start | bytes 262144 | tf_op jit(solution)/shard_map/sum_partials/all_to_all | solution.py:172
  85.0 7.8 %collective-permute-start.1 = (bf16[128,256]{1,0:T(8,128)(2,1)S(1)}, bf16[128,256]{1,0:T(8,128)(2,1)S(1)}, u32[]{:S(2)}, u32[]{:S(2)}) collective-permute-start(bf16[128,256]{1,0:T(8,128)(2,1)S(1)} %copy-done.2), channel_id=1, source_target_pairs={{0,2},{1,3},{2,0},{3,1},{4,6},{5,7},{6,4},{7,5},{8,10},{9,11},{10,... | collective-permute-start | bytes 196616 | tf_op jit(solution)/shard_map/partner_cotangent/ppermute | solution.py:175
  92.8 2.9 %collective-permute-done.1.partner_ref = bf16[128,256]{1,0:T(8,128)(2,1)S(1)} collective-permute-done((bf16[128,256]{1,0:T(8,128)(2,1)S(1)}, bf16[128,256]{1,0:T(8,128)(2,1)S(1)}, u32[]{:S(2)}, u32[]{:S(2)}) %collective-permute-start.1) | collective-permute-done | bytes 65568 | tf_op jit(solution)/shard_map/partner_cotangent/ppermute | solution.py:175
  95.8 0.0 all-to-all-done.3.halves_ref
  95.8 0.9 shard_map.86
  96.6 18.6 %all_to_all.43.own_ref = bf16[8,288,128]{2,1,0:T(8,128)(2,1)S(1)} all-to-all(bf16[8,288,128]{2,1,0:T(8,128)(2,1)S(1)} %get-tuple-element.12), channel_id=1, replica_groups={{0,4,8,12,16,20,24,28},{1,5,9,13,17,21,25,29},{2,6,10,14,18,22,26,30},{..., dimensions={0} | all-to-all | bytes 1179648 | tf_op jit(solution)/shard_map/gather_grads/all_to_all | solution.py:172
  115.2 1.9 %collective-permute-start.2 = (bf16[8,288,128]{2,1,0:T(8,128)(2,1)S(1)}, bf16[8,288,128]{2,1,0:T(8,128)(2,1)S(1)}, u32[]{:S(2)}, u32[]{:S(2)}) collective-permute-start(bf16[8,288,128]{2,1,0:T(8,128)(2,1)S(1)} %all_to_all.43.own_ref), channel_id=1, source_target_pairs={{0,1},{1,0},{2,3},{3,2},{4,5},{5,4},{6,7},{7,6},{8,9},{9,8},{10,11... | collective-permute-start | bytes 1769480 | tf_op jit(solution)/shard_map/gather_grads/ppermute | solution.py:199
  117.2 2.0 %collective-permute-done.2.other_ref = bf16[8,288,128]{2,1,0:T(8,128)(2,1)S(1)} collective-permute-done((bf16[8,288,128]{2,1,0:T(8,128)(2,1)S(1)}, bf16[8,288,128]{2,1,0:T(8,128)(2,1)S(1)}, u32[]{:S(2)}, u32[]{:S(2)}) %collective-permute-start.2) | collective-permute-done | bytes 589856 | tf_op jit(solution)/shard_map/gather_grads/ppermute | solution.py:199
  119.1 1.8 %shard_map.87 = bf16[4,1056,128]{2,1,0:T(8,128)(2,1)S(1)} custom-call(s32[2,32]{1,0:T(2,128)S(1)} %bitcast.13, s32[32]{0:T(128)S(1)} %bitcast.15, bf16[8,288,128]{2,1,0:T(8,128)(2,1)S(1)} %all_to_all.43.own_ref, bf16[8,288,128]{2,1,0:T(8,128)(2,1)S(1)} %collective-permute-done.2.other_ref, bf16[32,2,128,128]{3,2,1,0:T(8,128)(2,1)S(1)} %bitcast.11), custom_call_target="tpu_custom_call" | custom-call | tf_op jit(solution)/shard_map/pallas_call | solution.py:200
  120.9 19.2 %all_to_all.44.arrived_ref = bf16[4,1056,128]{2,1,0:T(8,128)(2,1)S(1)} all-to-all(bf16[4,1056,128]{2,1,0:T(8,128)(2,1)S(1)} %shard_map.87), channel_id=1, replica_groups={{0,32,256,288},{64,96,320,352},{128,160,384,416},{192,224,448,480},{512..., dimensions={0} | all-to-all | bytes 2162688 | tf_op jit(solution)/shard_map/sum_terms/all_to_all | solution.py:172
  140.1 0.1 sum_terms.1
  140.2 17.3 %all_to_all.45.parts_ref = bf16[8,160,128]{2,1,0:T(8,128)(2,1)S(1)} all-to-all(bf16[8,160,128]{2,1,0:T(8,128)(2,1)S(1)} %sum_terms.1), channel_id=1, replica_groups={{0,64,128,192,512,576,640,704},{32,96,160,224,544,608,672,736},{256,320..., dimensions={0} | all-to-all | bytes 655360 | tf_op jit(solution)/shard_map/sum_terms/all_to_all | solution.py:172
  157.6 0.7 shard_map.88
  158.3 11.5 %all_to_all.46 = f32[8,32,128]{2,1,0:T(8,128)S(1)} all-to-all(f32[8,32,128]{2,1,0:T(8,128)S(1)} %get-tuple-element.14), channel_id=1, replica_groups={{0,4,8,12,16,20,24,28},{1,5,9,13,17,21,25,29},{2,6,10,14,18,22,26,30},{..., dimensions={0} | all-to-all | bytes 262144 | tf_op jit(solution)/shard_map/gather_weight_grad/all_to_all | solution.py:172
  169.8 0.7 copy.10
  (5 shorter events, 0.0 us)
Async XLA Ops:
  0.6 0.8 copy-start.3
  32.6 14.9 %copy-start = (bf16[1,1,32,2,128,128]{5,4,3,2,1,0:T(8,128)(2,1)S(1)}, bf16[1,1,32,2,128,128]{5,4,3,2,1,0:T(8,128)(2,1)}, u32[]{:S(2)}) copy-start(bf16[1,1,32,2,128,128]{5,4,3,2,1,0:T(8,128)(2,1)} %param.9) | copy-start | bytes 6291460
  32.6 14.9 %copy-start.4 = (s32[1,1,32,2]{2,3,1,0:T(2,128)S(1)}, s32[1,1,32,2]{2,3,1,0:T(2,128)}, u32[]{:S(2)}) copy-start(s32[1,1,32,2]{2,3,1,0:T(2,128)} %param.10) | copy-start | bytes 772
  32.6 14.8 %copy-start.5 = (s32[1,1,32]{2,1,0:T(1,128)S(1)}, s32[1,1,32]{2,1,0:T(1,128)}, u32[]{:S(2)}) copy-start(s32[1,1,32]{2,1,0:T(1,128)} %param.11) | copy-start | bytes 388
  49.1 3.8 %collective-permute-start = (bf16[16,128,128]{2,1,0:T(8,128)(2,1)S(1)}, bf16[16,128,128]{2,1,0:T(8,128)(2,1)S(1)}, u32[]{:S(2)}, u32[]{:S(2)}) collective-permute-start(bf16[16,128,128]{2,1,0:T(8,128)(2,1)S(1)} %get-tuple-element.10), channel_id=1, source_target_pairs={{0,1},{1,0},{2,3},{3,2},{4,5},{5,4},{6,7},{7,6},{8,9},{9,8},{10,11... | collective-permute-start | bytes 1572872 | tf_op jit(solution)/shard_map/sum_partials/ppermute | solution.py:188
  53.0 32.0 %copy-start.2 = (bf16[128,256]{1,0:T(8,128)(2,1)S(1)}, bf16[128,256]{1,0:T(8,128)(2,1)}, u32[]{:S(2)}) copy-start(bf16[128,256]{1,0:T(8,128)(2,1)} %cotangent_ref.1) | copy-start | bytes 196612
  53.0 42.7 %copy-start.1 = (bf16[128,256]{1,0:T(8,128)(2,1)S(1)}, bf16[128,256]{1,0:T(8,128)(2,1)}, u32[]{:S(2)}) copy-start(bf16[128,256]{1,0:T(8,128)(2,1)} %weight_ref.1) | copy-start | bytes 196612
  77.3 18.4 %all-to-all-start.3 = ((bf16[4,128,128]{2,1,0:T(8,128)(2,1)}), bf16[4,128,128]{2,1,0:T(8,128)(2,1)S(1)}, u32[]{:S(2)}, u32[]{:S(2)}) async-start(bf16[4,128,128]{2,1,0:T(8,128)(2,1)} %sum_partials.1), calls=%async_computation.3 | async-start | bytes 262144 | tf_op jit(solution)/shard_map/sum_partials/all_to_all | solution.py:172
  85.0 10.8 %collective-permute-start.1 = (bf16[128,256]{1,0:T(8,128)(2,1)S(1)}, bf16[128,256]{1,0:T(8,128)(2,1)S(1)}, u32[]{:S(2)}, u32[]{:S(2)}) collective-permute-start(bf16[128,256]{1,0:T(8,128)(2,1)S(1)} %copy-done.2), channel_id=1, source_target_pairs={{0,2},{1,3},{2,0},{3,1},{4,6},{5,7},{6,4},{7,5},{8,10},{9,11},{10,... | collective-permute-start | bytes 196616 | tf_op jit(solution)/shard_map/partner_cotangent/ppermute | solution.py:175
  115.2 3.9 %collective-permute-start.2 = (bf16[8,288,128]{2,1,0:T(8,128)(2,1)S(1)}, bf16[8,288,128]{2,1,0:T(8,128)(2,1)S(1)}, u32[]{:S(2)}, u32[]{:S(2)}) collective-permute-start(bf16[8,288,128]{2,1,0:T(8,128)(2,1)S(1)} %all_to_all.43.own_ref), channel_id=1, source_target_pairs={{0,1},{1,0},{2,3},{3,2},{4,5},{5,4},{6,7},{7,6},{8,9},{9,8},{10,11... | collective-permute-start | bytes 1769480 | tf_op jit(solution)/shard_map/gather_grads/ppermute | solution.py:199
where the time goes:
time: 171 us; the launch traced here: 170 us
  blocking collectives  136 us (80%)
  starting transfers between devices  19.3 us (11%)
  waiting for transfers between devices  6.78 us (4%)
  Pallas kernels  6 us (4%)
    all_to_all x7, blocking collectives, exchange(): lax.all_to_all(block, axis, 0, 0, axis_index_groups=index_groups, tiled=T...  136 us
    ppermute x1, starting transfers between devices, local(): partner = lax.ppermute(cotangent, 'rep', swap_y)  7.83 us
    all_to_all x1, starting transfers between devices, exchange(): lax.all_to_all(block, axis, 0, 0, axis_index_groups=index_groups, tiled=T...  7.65 us
  transfers between devices with their start and end apart: 4, of which 3 were waited for; matrix products, arithmetic and copies ran while one was open for 0% of the time, Pallas kernels for 0%

commit v1 on v0

--- a/solution.py
+++ b/solution.py
@@ -178,6 +178,7 @@
         band = exchange(copies, "blk", far_blocks)
         (copies,) = call(spread, [VMEM], [shape(nears, fars, side, width)])(band)
         gathered = exchange(copies, "blk", near_blocks)
+        gathered, partner = lax.optimization_barrier((gathered, partner))
     kept, sent = call(
         forward_tiles,
         [SMEM, SMEM, VMEM, VMEM],

time: 171 us -> 172 us (level)
  waiting for transfers between devices: 6.78 us -> 15.4 us
  starting transfers between devices: 19.3 us -> 13.7 us
  blocking collectives: 136 us -> 133 us
    ppermute x1, waiting for transfers between devices: 2.93 us -> 11.6 us  [local(): partner = lax.ppermute(cotangent, 'rep', swap_y)]
    all_to_all x1, starting transfers between devices: 7.65 us -> 3.8 us  [exchange(): lax.all_to_all(block, axis, 0, 0, axis_index_groups=index_groups, tiled=T...]
    all_to_all x7, blocking collectives: 136 us -> 133 us  [exchange(): lax.all_to_all(block, axis, 0, 0, axis_index_groups=index_groups, tiled=T...]
    ppermute x1, starting transfers between devices: 7.83 us -> 6.02 us  [local(): partner = lax.ppermute(cotangent, 'rep', swap_y)]
where the time goes in v1:
time: 172 us; the launch traced here: 171 us
  blocking collectives  133 us (77%)
  waiting for transfers between devices  15.4 us (9%)
  starting transfers between devices  13.7 us (8%)
  Pallas kernels  6.32 us (4%)
    all_to_all x7, blocking collectives, exchange(): lax.all_to_all(block, axis, 0, 0, axis_index_groups=index_groups, tiled=T...  133 us
    ppermute x1, waiting for transfers between devices, local(): partner = lax.ppermute(cotangent, 'rep', swap_y)  11.6 us
    ppermute x1, starting transfers between devices, local(): partner = lax.ppermute(cotangent, 'rep', swap_y)  6.02 us
    all_to_all x1, starting transfers between devices, exchange(): lax.all_to_all(block, axis, 0, 0, axis_index_groups=index_groups, tiled=T...  3.8 us
  transfers between devices with their start and end apart: 4, of which 3 were waited for; matrix products, arithmetic and copies ran while one was open for 0% of the time, Pallas kernels for 0%

profile of v1, /device:TPU:2, one launch (start us, length us, event | category | flops | bytes accessed | tf_op | source)
XLA Modules:
  0.0 170.9 jit_solution(14390057038403252448)
XLA Ops:
  0.6 0.0 copy-start.3
  0.6 0.7 copy-done.3
  1.4 31.0 %all_to_all.40.block_ref = bf16[8,128,128]{2,1,0:T(8,128)(2,1)S(1)} all-to-all(bf16[8,128,128]{2,1,0:T(8,128)(2,1)S(1)} %gather_features.2), channel_id=1, replica_groups={{0,64,128,192,512,576,640,704},{32,96,160,224,544,608,672,736},{256,320..., dimensions={0} | all-to-all | bytes 524288 | tf_op jit(solution)/shard_map/gather_features/all_to_all | solution.py:172
  32.5 1.1 gather_features.3
  33.6 3.8 %all-to-all-start.1 = ((bf16[4,8,128,128]{3,2,1,0:T(8,128)(2,1)}), bf16[4,8,128,128]{3,2,1,0:T(8,128)(2,1)S(1)}, u32[]{:S(2)}, u32[]{:S(2)}) async-start(bf16[4,8,128,128]{3,2,1,0:T(8,128)(2,1)} %gather_features.3), calls=%async_computation.1 | async-start | bytes 2097152 | tf_op jit(solution)/shard_map/gather_features/all_to_all | solution.py:172
  37.4 0.0 copy-done.2
  37.4 6.0 %collective-permute-start = (bf16[128,256]{1,0:T(8,128)(2,1)S(1)}, bf16[128,256]{1,0:T(8,128)(2,1)S(1)}, u32[]{:S(2)}, u32[]{:S(2)}) collective-permute-start(bf16[128,256]{1,0:T(8,128)(2,1)S(1)} %copy-done.2), channel_id=1, source_target_pairs={{0,2},{1,3},{2,0},{3,1},{4,6},{5,7},{6,4},{7,5},{8,10},{9,11},{10,... | collective-permute-start | bytes 196616 | tf_op jit(solution)/shard_map/partner_cotangent/ppermute | solution.py:175
  43.4 11.6 %collective-permute-done.partner_ref = bf16[128,256]{1,0:T(8,128)(2,1)S(1)} collective-permute-done((bf16[128,256]{1,0:T(8,128)(2,1)S(1)}, bf16[128,256]{1,0:T(8,128)(2,1)S(1)}, u32[]{:S(2)}, u32[]{:S(2)}) %collective-permute-start) | collective-permute-done | bytes 65568 | tf_op jit(solution)/shard_map/partner_cotangent/ppermute | solution.py:175
  55.0 0.0 all-to-all-done.1.features_ref
  55.0 0.0 copy-done
  55.0 0.0 copy-done.4
  55.0 0.0 copy-done.5
  55.0 1.6 shard_map.85
  56.6 1.9 %collective-permute-start.1 = (bf16[16,128,128]{2,1,0:T(8,128)(2,1)S(1)}, bf16[16,128,128]{2,1,0:T(8,128)(2,1)S(1)}, u32[]{:S(2)}, u32[]{:S(2)}) collective-permute-start(bf16[16,128,128]{2,1,0:T(8,128)(2,1)S(1)} %get-tuple-element.13), channel_id=1, source_target_pairs={{0,1},{1,0},{2,3},{3,2},{4,5},{5,4},{6,7},{7,6},{8,9},{9,8},{10,11... | collective-permute-start | bytes 1572872 | tf_op jit(solution)/shard_map/sum_partials/ppermute | solution.py:189
  58.5 1.9 %collective-permute-done.1 = bf16[16,128,128]{2,1,0:T(8,128)(2,1)S(1)} collective-permute-done((bf16[16,128,128]{2,1,0:T(8,128)(2,1)S(1)}, bf16[16,128,128]{2,1,0:T(8,128)(2,1)S(1)}, u32[]{:S(2)}, u32[]{:S(2)}) %collective-permute-start.1) | collective-permute-done | bytes 524320 | tf_op jit(solution)/shard_map/sum_partials/ppermute | solution.py:189
  60.4 0.1 add_convert_fusion
  60.6 0.0 copy-start.1
  60.6 23.6 %all_to_all.41.parts_ref = bf16[16,128,128]{2,1,0:T(8,128)(2,1)S(1)} all-to-all(bf16[16,128,128]{2,1,0:T(8,128)(2,1)S(1)} %add_convert_fusion), channel_id=1, replica_groups={{0,4,8,12,16,20,24,28},{1,5,9,13,17,21,25,29},{2,6,10,14,18,22,26,30},{..., dimensions={0} | all-to-all | bytes 1048576 | tf_op jit(solution)/shard_map/sum_partials/all_to_all | solution.py:172
  84.1 0.1 sum_partials.1
  84.2 11.5 %all_to_all.42.halves_ref = bf16[4,128,128]{2,1,0:T(8,128)(2,1)S(1)} all-to-all(bf16[4,128,128]{2,1,0:T(8,128)(2,1)S(1)} %sum_partials.1), channel_id=1, replica_groups={{0,2},{1,3},{4,6},{5,7},{8,10},{9,11},{12,14},{13,15},{16,18},{17,19},{..., dimensions={0} | all-to-all | bytes 262144 | tf_op jit(solution)/shard_map/sum_partials/all_to_all | solution.py:172
  95.7 0.0 copy-done.1
  95.7 0.9 shard_map.86
  96.6 19.1 %all_to_all.43.own_ref = bf16[8,288,128]{2,1,0:T(8,128)(2,1)S(1)} all-to-all(bf16[8,288,128]{2,1,0:T(8,128)(2,1)S(1)} %get-tuple-element.16), channel_id=1, replica_groups={{0,4,8,12,16,20,24,28},{1,5,9,13,17,21,25,29},{2,6,10,14,18,22,26,30},{..., dimensions={0} | all-to-all | bytes 1179648 | tf_op jit(solution)/shard_map/gather_grads/all_to_all | solution.py:172
  115.7 1.9 %collective-permute-start.2 = (bf16[8,288,128]{2,1,0:T(8,128)(2,1)S(1)}, bf16[8,288,128]{2,1,0:T(8,128)(2,1)S(1)}, u32[]{:S(2)}, u32[]{:S(2)}) collective-permute-start(bf16[8,288,128]{2,1,0:T(8,128)(2,1)S(1)} %all_to_all.43.own_ref), channel_id=1, source_target_pairs={{0,1},{1,0},{2,3},{3,2},{4,5},{5,4},{6,7},{7,6},{8,9},{9,8},{10,11... | collective-permute-start | bytes 1769480 | tf_op jit(solution)/shard_map/gather_grads/ppermute | solution.py:200
  117.6 2.0 %collective-permute-done.2.other_ref = bf16[8,288,128]{2,1,0:T(8,128)(2,1)S(1)} collective-permute-done((bf16[8,288,128]{2,1,0:T(8,128)(2,1)S(1)}, bf16[8,288,128]{2,1,0:T(8,128)(2,1)S(1)}, u32[]{:S(2)}, u32[]{:S(2)}) %collective-permute-start.2) | collective-permute-done | bytes 589856 | tf_op jit(solution)/shard_map/gather_grads/ppermute | solution.py:200
  119.6 1.8 %shard_map.87 = bf16[4,1056,128]{2,1,0:T(8,128)(2,1)S(1)} custom-call(s32[2,32]{1,0:T(2,128)S(1)} %bitcast.13, s32[32]{0:T(128)S(1)} %bitcast.15, bf16[8,288,128]{2,1,0:T(8,128)(2,1)S(1)} %all_to_all.43.own_ref, bf16[8,288,128]{2,1,0:T(8,128)(2,1)S(1)} %collective-permute-done.2.other_ref, bf16[32,2,128,128]{3,2,1,0:T(8,128)(2,1)S(1)} %bitcast.11), custom_call_target="tpu_custom_call" | custom-call | tf_op jit(solution)/shard_map/pallas_call | solution.py:201
  121.4 18.8 %all_to_all.44.arrived_ref = bf16[4,1056,128]{2,1,0:T(8,128)(2,1)S(1)} all-to-all(bf16[4,1056,128]{2,1,0:T(8,128)(2,1)S(1)} %shard_map.87), channel_id=1, replica_groups={{0,32,256,288},{64,96,320,352},{128,160,384,416},{192,224,448,480},{512..., dimensions={0} | all-to-all | bytes 2162688 | tf_op jit(solution)/shard_map/sum_terms/all_to_all | solution.py:172
  140.2 0.1 sum_terms.1
  140.3 17.8 %all_to_all.45.parts_ref = bf16[8,160,128]{2,1,0:T(8,128)(2,1)S(1)} all-to-all(bf16[8,160,128]{2,1,0:T(8,128)(2,1)S(1)} %sum_terms.1), channel_id=1, replica_groups={{0,64,128,192,512,576,640,704},{32,96,160,224,544,608,672,736},{256,320..., dimensions={0} | all-to-all | bytes 655360 | tf_op jit(solution)/shard_map/sum_terms/all_to_all | solution.py:172
  158.1 0.7 shard_map.88
  158.8 11.4 %all_to_all.46 = f32[8,32,128]{2,1,0:T(8,128)S(1)} all-to-all(f32[8,32,128]{2,1,0:T(8,128)S(1)} %get-tuple-element.18), channel_id=1, replica_groups={{0,4,8,12,16,20,24,28},{1,5,9,13,17,21,25,29},{2,6,10,14,18,22,26,30},{..., dimensions={0} | all-to-all | bytes 262144 | tf_op jit(solution)/shard_map/gather_weight_grad/all_to_all | solution.py:172
  170.3 0.7 copy.10
  (5 shorter events, 0.0 us)
Async XLA Ops:
  0.6 0.8 copy-start.3
  32.5 4.9 %copy-start.2 = (bf16[128,256]{1,0:T(8,128)(2,1)S(1)}, bf16[128,256]{1,0:T(8,128)(2,1)}, u32[]{:S(2)}) copy-start(bf16[128,256]{1,0:T(8,128)(2,1)} %cotangent_ref.1) | copy-start | bytes 196612
  33.6 21.4 %copy-start = (bf16[1,1,32,2,128,128]{5,4,3,2,1,0:T(8,128)(2,1)S(1)}, bf16[1,1,32,2,128,128]{5,4,3,2,1,0:T(8,128)(2,1)}, u32[]{:S(2)}) copy-start(bf16[1,1,32,2,128,128]{5,4,3,2,1,0:T(8,128)(2,1)} %param.9) | copy-start | bytes 6291460
  33.6 21.4 %copy-start.4 = (s32[1,1,32,2]{2,3,1,0:T(2,128)S(1)}, s32[1,1,32,2]{2,3,1,0:T(2,128)}, u32[]{:S(2)}) copy-start(s32[1,1,32,2]{2,3,1,0:T(2,128)} %param.10) | copy-start | bytes 772
  33.6 21.4 %copy-start.5 = (s32[1,1,32]{2,1,0:T(1,128)S(1)}, s32[1,1,32]{2,1,0:T(1,128)}, u32[]{:S(2)}) copy-start(s32[1,1,32]{2,1,0:T(1,128)} %param.11) | copy-start | bytes 388
  33.6 21.4 %all-to-all-start.1 = ((bf16[4,8,128,128]{3,2,1,0:T(8,128)(2,1)}), bf16[4,8,128,128]{3,2,1,0:T(8,128)(2,1)S(1)}, u32[]{:S(2)}, u32[]{:S(2)}) async-start(bf16[4,8,128,128]{3,2,1,0:T(8,128)(2,1)} %gather_features.3), calls=%async_computation.1 | async-start | bytes 2097152 | tf_op jit(solution)/shard_map/gather_features/all_to_all | solution.py:172
  37.4 17.6 %collective-permute-start = (bf16[128,256]{1,0:T(8,128)(2,1)S(1)}, bf16[128,256]{1,0:T(8,128)(2,1)S(1)}, u32[]{:S(2)}, u32[]{:S(2)}) collective-permute-start(bf16[128,256]{1,0:T(8,128)(2,1)S(1)} %copy-done.2), channel_id=1, source_target_pairs={{0,2},{1,3},{2,0},{3,1},{4,6},{5,7},{6,4},{7,5},{8,10},{9,11},{10,... | collective-permute-start | bytes 196616 | tf_op jit(solution)/shard_map/partner_cotangent/ppermute | solution.py:175
  56.6 3.8 %collective-permute-start.1 = (bf16[16,128,128]{2,1,0:T(8,128)(2,1)S(1)}, bf16[16,128,128]{2,1,0:T(8,128)(2,1)S(1)}, u32[]{:S(2)}, u32[]{:S(2)}) collective-permute-start(bf16[16,128,128]{2,1,0:T(8,128)(2,1)S(1)} %get-tuple-element.13), channel_id=1, source_target_pairs={{0,1},{1,0},{2,3},{3,2},{4,5},{5,4},{6,7},{7,6},{8,9},{9,8},{10,11... | collective-permute-start | bytes 1572872 | tf_op jit(solution)/shard_map/sum_partials/ppermute | solution.py:189
  60.6 35.1 %copy-start.1 = (bf16[128,256]{1,0:T(8,128)(2,1)S(1)}, bf16[128,256]{1,0:T(8,128)(2,1)}, u32[]{:S(2)}) copy-start(bf16[128,256]{1,0:T(8,128)(2,1)} %weight_ref.1) | copy-start | bytes 196612
  115.7 3.9 %collective-permute-start.2 = (bf16[8,288,128]{2,1,0:T(8,128)(2,1)S(1)}, bf16[8,288,128]{2,1,0:T(8,128)(2,1)S(1)}, u32[]{:S(2)}, u32[]{:S(2)}) collective-permute-start(bf16[8,288,128]{2,1,0:T(8,128)(2,1)S(1)} %all_to_all.43.own_ref), channel_id=1, source_target_pairs={{0,1},{1,0},{2,3},{3,2},{4,5},{5,4},{6,7},{7,6},{8,9},{9,8},{10,11... | collective-permute-start | bytes 1769480 | tf_op jit(solution)/shard_map/gather_grads/ppermute | solution.py:200
